TPU v7x, 32 devices: a whole 2x2x4 slice. The times are simulated.
32 devices in a mesh: groups: 2 (over y), tm: 4 (over z), param: 4 (over x, core).
Axes of the slice: x: 2, y: 2, z: 4, core: 2. Of those that a mesh axis runs over, the one named last changes fastest.
Arguments:
- design: float32 [3, 512, 40960], P(None, ('groups', 'tm'), 'param'), parts along dimension 1, may hold values from -0.03125 to 0.03125
- filter_taps: float32 [3, 512], replicated, may hold values from -0.25 to 0.25
- probes: float32 [40960, 256], P('param', ('groups', 'tm')), parts along dimension 1, may hold values from -6 to 6
Outputs:
- normal_product: float32 [40960, 256], P('param', ('groups', 'tm')), parts along dimension 1
There are 2 independent parts, one for each index of `groups`. A program takes and returns all parts, laid end to end along the dimension named above; an argument that names none is the same for every part. Nothing has to cross between parts.
All inputs are finite; a program needn't handle non-finite values.
Results may differ from a plain program's by a relative error of at most 0.000071.
Values sent between devices are 32-bit elements; how exact they have to be, the bound alone decides.
A program may use at most 128 MiB of HBM per device.

v0:
```python
import math

import jax
import jax.numpy as jnp
import numpy as np
from jax import lax
from jax.sharding import PartitionSpec as P


def passed_along(value, axis, by):
    length = lax.axis_size(axis)
    pairs = [(i, i + by) for i in range(length) if 0 <= i + by < length]
    return lax.ppermute(value, axis, pairs)


def block_taps(filter_taps, epochs, block_total, forward):
    shape = (block_total, epochs, epochs)
    distance = lax.broadcasted_iota(jnp.int32, shape, 0)
    source = lax.broadcasted_iota(jnp.int32, shape, 1)
    target = lax.broadcasted_iota(jnp.int32, shape, 2)
    if forward:
        lag_index = distance * epochs + target - source
    else:
        lag_index = distance * epochs + source - target
    tap_count = filter_taps.shape[1]
    inside = (lag_index >= 0) & (lag_index < tap_count)
    values = jnp.take(filter_taps, jnp.clip(lag_index, 0, tap_count - 1), axis=1)
    return jnp.where(inside[None], values, 0.0)


def apply_blocks(stacked, matrices):
    return jnp.einsum("ckdbe,cdef->ckbf", stacked, matrices, precision=lax.Precision.HIGHEST)


def body(design, filter_taps, probes):
    highest = lax.Precision.HIGHEST
    components, epochs, coefficients = design.shape
    tap_count = filter_taps.shape[1]
    blocks_back = (tap_count - 1 + epochs - 1) // epochs
    block_total = blocks_back + 1
    block_width = math.gcd(coefficients, 512)
    block_count = coefficients // block_width
    forward_taps = block_taps(filter_taps, epochs, block_total, True)
    backward_taps = block_taps(filter_taps, epochs, block_total, False)
    columns = lax.all_gather(probes, "tm", axis=1, tiled=True)

    def accumulate(step_index, running):
        start = step_index * block_width
        design_block = lax.dynamic_slice_in_dim(design, start, block_width, 2)
        column_block = lax.dynamic_slice_in_dim(columns, start, block_width, 0)
        return running + jnp.einsum("ctp,pk->ckt", design_block, column_block, precision=highest)

    initial = jnp.zeros((components, columns.shape[1], epochs), jnp.float32)
    projected = lax.fori_loop(0, block_count, accumulate, initial)
    projected = lax.psum_scatter(projected, "param", scatter_dimension=1, tiled=True)
    probe_count = projected.shape[1]
    before = [passed_along(projected, "tm", distance) for distance in range(blocks_back, 0, -1)]
    extended = jnp.stack(before + [projected], axis=2)
    pick_forward = np.array([[blocks_back - d] for d in range(block_total)], np.int32)
    filtered = apply_blocks(extended[:, :, pick_forward], forward_taps)
    filtered = filtered.reshape(components, probe_count, epochs)
    trailing = [passed_along(filtered, "tm", -distance) for distance in range(1, blocks_back + 1)]
    extended = jnp.stack([filtered] + trailing, axis=2)
    weighted = apply_blocks(extended[:, :, :, None], backward_taps)
    weighted = weighted.reshape(components, probe_count, epochs)
    weighted = lax.all_gather(weighted, "param", axis=1, tiled=True)

    def block_product(step_index):
        design_block = lax.dynamic_slice_in_dim(design, step_index * block_width, block_width, 2)
        return jnp.einsum("ctp,ckt->pk", design_block, weighted, precision=highest)

    stacked = lax.map(block_product, jnp.arange(block_count, dtype=jnp.int32))
    partial_value = stacked.reshape(coefficients, weighted.shape[1])
    result = lax.psum_scatter(partial_value, "tm", scatter_dimension=1, tiled=True)
    return result


def solution(mesh):
    in_specs = (P(None, ("groups", "tm"), "param"), P(), P("param", ("groups", "tm")))
    out_specs = P("param", ("groups", "tm"))
    return jax.shard_map(body, mesh=mesh, in_specs=in_specs, out_specs=out_specs, check_vma=False)
```

profile of v0, /device:TPU:0, one launch (start us, length us, event | category | flops | bytes accessed | tf_op | source)
XLA Modules:
  0.0 659.3 jit_solution(4134613164685531167)
XLA Ops:
  7.7 102.0 %all-gather.2.cloned.1.call-done = f32[10240,128]{0,1:T(8,128)} async-done(((f32[10240,32]{0,1:T(8,128)}), f32[10240,128]{0,1:T(8,128)}) %all-gather.2.cloned.1.call-update) | async-done | bytes 5242896 | tf_op jit(solution)/shard_map/all_gather | solution.py:45
  109.7 32.3 %while.25 = (s32[]{:T(128)}, f32[3,128,64]{1,2,0:T(8,128)S(1)}, f32[10240,128]{0,1:T(8,128)}, f32[3,64,10240]{2,1,0:T(8,128)}, s32[]{:T(128)}, /*index=5*/s32[]{:T(128)}, s32[]{:T(128)}, s32[]{:T(128)}) while((s32[]{:T(128)}, f32[3,128,64]{1,2,0:T(8,128)S(1)}, f32[10240,128]{0,1:T(8,128)}, f32[3,64,10240]{2,1,0:T(8,128)}, ...), condition=%wide.region_1.2_spmd.clone, body=%wide.region_0.1_spmd.clone.sunk | while | flops 151044096 | bytes 853644 | solution.py:54
  109.7 1.6 fusion.37
  111.3 1.6 fusion.37
  113.0 1.6 fusion.37
  114.6 1.6 fusion.37
  116.2 1.6 fusion.37
  117.8 1.6 fusion.37
  119.4 1.6 fusion.37
  121.0 1.6 fusion.37
  122.7 1.6 fusion.37
  124.3 1.6 fusion.37
  125.9 1.6 fusion.37
  127.5 1.6 fusion.37
  129.1 1.6 fusion.37
  130.7 1.6 fusion.37
  132.4 1.6 fusion.37
  134.0 1.6 fusion.37
  135.6 1.6 fusion.37
  137.2 1.6 fusion.37
  138.8 1.6 fusion.37
  140.4 1.6 fusion.37
  142.0 0.8 copy.25
  144.8 28.6 %all-reduce.3.cloned.1.call-done = f32[3,128,64]{2,0,1:T(4,128)} async-done(((f32[3,128,64]{2,0,1:T(4,128)}), f32[3,128,64]{2,0,1:T(4,128)}) %all-reduce.3.cloned.1.call-update) | async-done | bytes 98320
  173.4 0.9 constant_dynamic-slice_fusion
  175.1 121.7 %gather_fusion.1 = f32[36864,3]{1,0:T(8,128)} fusion(f32[3,512]{0,1:T(8,128)S(1)} %copy.26, s32[36864]{0:T(1024)S(1)} %broadcast_clamp_fusion.1), kind=kCustom, calls=%fused_computation.clone | custom fusion | bytes 1032192 | tf_op jit(solution)/shard_map/jit(_take)/gather | solution.py:27
  296.8 11.0 %copy.27 = f32[9,64,64,3]{2,1,3,0:T(8,128)S(1)} copy(f32[9,64,64,3]{3,2,1,0:T(8,128)} %bitcast.74) | data formatting | bytes 884736 | tf_op jit(solution)/shard_map/jit(_take)/gather | solution.py:27
  308.0 5.2 collective-permute-start.1
  313.2 1.3 collective-permute-start.2
  314.5 2.5 collective-permute-start.3
  317.2 1.7 collective-permute-done.3
  318.9 0.9 bitcast_dynamic-update-slice_fusion
  319.8 0.9 gather_fusion
  321.5 1.3 collective-permute-start.4
  322.8 121.7 %gather_fusion.2 = f32[36864,3]{1,0:T(8,128)} fusion(f32[3,512]{0,1:T(8,128)S(1)} %copy.26, s32[36864]{0:T(1024)S(1)} %broadcast_clamp_fusion), kind=kCustom, calls=%fused_computation.1.clone | custom fusion | bytes 1032192 | tf_op jit(solution)/shard_map/jit(_take)/gather | solution.py:27
  444.5 11.0 %copy.30 = f32[9,64,64,3]{2,1,3,0:T(8,128)S(1)} copy(f32[9,64,64,3]{3,2,1,0:T(8,128)} %bitcast.73) | data formatting | bytes 884736 | tf_op jit(solution)/shard_map/jit(_take)/gather | solution.py:27
  455.6 1.3 collective-permute-start.5
  456.9 1.3 collective-permute-start.6
  458.9 4.8 collective-permute-done.5
  463.7 2.5 collective-permute-done.6
  467.1 5.6 all_gather.7
  472.8 82.8 %while.24 = (s32[]{:T(128)}, f32[20,512,128]{2,1,0:T(8,128)}, s32[20]{0:T(128)S(1)}, f32[3,64,10240]{2,1,0:T(8,128)}, f32[3,128,64]{1,2,0:T(8,128)S(1)}, /*index=5*/s32[]{:T(128)}, s32[1]{0:T(128)}, s32[]{:T(128)}, s32[]{:T(128)}) while((s32[]{:T(128)}, f32[20,512,128]{2,1,0:T(8,128)}, s32[20]{0:T(128)S(1)}, f32[3,64,10240]{2,1,0:T(8,128)}, ...), condition=%wide.region_4.6_spmd, body=%wide.region_3.5_spmd.sunk | while | flops 150994944 | bytes 754331 | solution.py:72
  474.2 2.8 fusion.34
  478.3 2.8 fusion.34
  482.5 2.8 fusion.34
  486.6 2.8 fusion.34
  490.8 2.8 fusion.34
  494.9 2.8 fusion.34
  499.0 2.8 fusion.34
  503.2 2.8 fusion.34
  507.3 2.8 fusion.34
  511.4 2.8 fusion.34
  515.6 2.8 fusion.34
  519.7 2.8 fusion.34
  523.9 2.8 fusion.34
  528.0 2.8 fusion.34
  532.2 2.8 fusion.34
  536.3 2.8 fusion.34
  540.4 2.8 fusion.34
  544.6 2.8 fusion.34
  548.7 2.8 fusion.34
  552.9 2.8 fusion.34
  555.7 5.9 copy.37
  561.5 91.2 %reduce-scatter.4.cloned.1.call-done = f32[32,10240]{1,0:T(8,128)} async-done(((f32[128,10240]{1,0:T(8,128)}), f32[32,10240]{1,0:T(8,128)}) %reduce-scatter.4.cloned.1.call-update) | async-done | bytes 1310736
  (71 shorter events, 19.1 us)
Async XLA Ops:
  6.5 136.9 %copy-start.2 = (u32[32]{0:T(128)S(1)}, u32[32]{0:T(128)}, u32[]{:S(2)}) copy-start(u32[32]{0:T(128)} %constant.76) | copy-start | bytes 388
  6.5 168.4 %copy-start.1 = (s32[9]{0:T(128)S(1)}, s32[9]{0:T(128)}, u32[]{:S(2)}) copy-start(s32[9]{0:T(128)} %constant.73) | copy-start | bytes 112
  6.5 168.4 %copy-start = (f32[3,512]{1,0:T(4,128)S(1)}, f32[3,512]{1,0:T(4,128)}, u32[]{:S(2)}) copy-start(f32[3,512]{1,0:T(4,128)} %param.12) | copy-start | bytes 18436
  6.5 103.2 %all-gather.2.cloned.1.call-start = ((), (), s32[]{:S(2)}) async-start(), calls=%async_computation.1 | async-start | bytes 6553600 | tf_op jit(solution)/shard_map/all_gather | solution.py:45
  7.3 166.1 %all-reduce.3.cloned.1.call-start = ((), (), s32[]{:S(2)}) async-start(), calls=%async_computation.3 | async-start | bytes 524288
  142.9 509.8 %reduce-scatter.4.cloned.1.call-start = ((), (), s32[]{:S(2)}) async-start(), calls=%async_computation.2 | async-start | bytes 6553600
  174.3 142.7 %collective-permute-start = (f32[3,32,64]{2,0,1:T(4,128)S(1)}, f32[3,32,64]{2,0,1:T(4,128)S(1)}, u32[]{:S(2)}, u32[]{:S(2)}) collective-permute-start(f32[3,32,64]{2,0,1:T(4,128)S(1)} %constant_dynamic-slice_fusion), channel_id=1, source_target_pairs={} | collective-permute-start | bytes 73736 | tf_op jit(solution)/shard_map/ppermute | solution.py:13
  308.0 9.2 %collective-permute-start.1 = (f32[3,32,64]{2,0,1:T(4,128)S(1)}, f32[3,32,64]{2,0,1:T(4,128)S(1)}, u32[]{:S(2)}, u32[]{:S(2)}) collective-permute-start(f32[3,32,64]{2,0,1:T(4,128)S(1)} %constant_dynamic-slice_fusion), channel_id=1, source_target_pairs={{0,12},{1,13},{2,14},{3,15},{16,28},{17,29},{18,30},{19,31}} | collective-permute-start | bytes 73736 | tf_op jit(solution)/shard_map/ppermute | solution.py:13
  313.2 4.0 collective-permute-start.2
  314.5 4.4 collective-permute-start.3
  321.5 137.3 %collective-permute-start.4 = (f32[3,32,64]{2,1,0:T(8,128)S(1)}, f32[3,32,64]{2,1,0:T(8,128)S(1)}, u32[]{:S(2)}, u32[]{:S(2)}) collective-permute-start(f32[3,32,64]{2,1,0:T(8,128)S(1)} %bitcast.77), channel_id=1, source_target_pairs={{4,0},{8,4},{12,8},{5,1},{9,5},{13,9},{6,2},{10,6},{14,10},{7,3},{... | collective-permute-start | bytes 73736 | tf_op jit(solution)/shard_map/ppermute | solution.py:13
  455.6 8.1 %collective-permute-start.5 = (f32[3,32,64]{2,1,0:T(8,128)S(1)}, f32[3,32,64]{2,1,0:T(8,128)S(1)}, u32[]{:S(2)}, u32[]{:S(2)}) collective-permute-start(f32[3,32,64]{2,1,0:T(8,128)S(1)} %bitcast.78), channel_id=1, source_target_pairs={{8,0},{12,4},{9,1},{13,5},{10,2},{14,6},{11,3},{15,7},{24,16},{28,... | collective-permute-start | bytes 73736 | tf_op jit(solution)/shard_map/ppermute | solution.py:13
  456.9 9.3 %collective-permute-start.6 = (f32[3,32,64]{2,1,0:T(8,128)S(1)}, f32[3,32,64]{2,1,0:T(8,128)S(1)}, u32[]{:S(2)}, u32[]{:S(2)}) collective-permute-start(f32[3,32,64]{2,1,0:T(8,128)S(1)} %bitcast.79), channel_id=1, source_target_pairs={{12,0},{13,1},{14,2},{15,3},{28,16},{29,17},{30,18},{31,19}} | collective-permute-start | bytes 73736 | tf_op jit(solution)/shard_map/ppermute | solution.py:13
  458.2 8.0 %collective-permute-start.7 = (f32[3,32,64]{2,1,0:T(8,128)S(1)}, f32[3,32,64]{2,1,0:T(8,128)S(1)}, u32[]{:S(2)}, u32[]{:S(2)}) collective-permute-start(f32[3,32,64]{2,1,0:T(8,128)S(1)} %bitcast.80), channel_id=1, source_target_pairs={} | collective-permute-start | bytes 73736 | tf_op jit(solution)/shard_map/ppermute | solution.py:13
Sparse Core Ops, SparseCore 0:
  8.9 100.7 all-gather.1
  143.0 30.3 all-reduce.2
  561.7 91.0 reduce-scatter.3
where the time goes:
time: 661 us; the launch traced here: 659 us
  local copies, waits for them, and re-layouts  289 us (44%)
  waiting for transfers between devices  232 us (35%)
  matrix products  89 us (13%)
  loops' own time  14.6 us (2%)
  starting transfers between devices  14.3 us (2%)
  between operations  14.2 us (2%)
    gather x4, local copies, waits for them, and re-layouts, block_taps(): jnp.take(filter_taps, jnp.clip(lag_index, 0, tap_count - 1), axis=1)  265 us
    unnamed x5, waiting for transfers between devices  121 us
    all_gather x1, waiting for transfers between devices, body(): columns = lax.all_gather(probes, 'tm', axis=1, tiled=True)  102 us
    dot_general x20, matrix products, block_product(): return jnp.einsum('ctp,ckt->pk', design_block, weighted, precision=highest)  55.6 us
    dot_general x20, matrix products, accumulate(): jnp.einsum('ctp,pk->ckt', design_block, column_block, precision=highest)  31.7 us
    ppermute x8, starting transfers between devices, passed_along(): return lax.ppermute(value, axis, pairs)  14.2 us
    another operation x1, loops' own time, body(): stacked = lax.map(block_product, jnp.arange(block_count, dtype=jnp.int32))  14 us
  transfers between devices with their start and end apart: 11, of which 6 were waited for; matrix products, arithmetic and copies ran while one was open for 41% of the time, Pallas kernels for 0%

commit v1 on v0

--- a/solution.py
+++ b/solution.py
@@ -1,9 +1,12 @@
+import functools
 import math
 
 import jax
 import jax.numpy as jnp
 import numpy as np
 from jax import lax
+from jax.experimental import pallas as pl
+from jax.experimental.pallas import tpu as pltpu
 from jax.sharding import PartitionSpec as P
 
 
@@ -75,7 +78,263 @@
     return result
 
 
+CHUNK = 8
+PIECES = 2
+MESH = pl.DeviceIdType.MESH
+
+
+def halves(value):
+    high = value.astype(jnp.bfloat16)
+    low = (value - high.astype(jnp.float32)).astype(jnp.bfloat16)
+    return high, low
+
+
+def across(left, right, precision=None):
+    return lax.dot_general(left, right, (((1,), (1,)), ((), ())), precision=precision, preferred_element_type=jnp.float32)
+
+
+def kernel(tm, param, components, design, taps, probes, out, raw, split, gathered, products, arrived, partials, signals,
+           normal, blocks, load_sem, probe_sem, out_sem, a_send, a_recv, b_send, b_recv, p_send, p_recv, t_send, t_recv):
+    rows, coefficients = raw.shape
+    epochs = rows // components
+    chunks = gathered.shape[0]
+    piece = coefficients // PIECES
+    z = lax.axis_index("tm")
+    q = lax.axis_index("param")
+    highest = lax.Precision.HIGHEST
+
+    tile = math.gcd(coefficients, 2048)
+    tiles = coefficients // tile
+    loads = [pltpu.make_async_copy(design.at[:, pl.ds(j * tile, tile)], raw.at[:, pl.ds(j * tile, tile)], load_sem.at[j]) for j in range(tiles)]
+    fetches = [pltpu.make_async_copy(probes.at[pl.ds(c * CHUNK, CHUNK)], gathered.at[c, z], probe_sem.at[c]) for c in range(chunks)]
+    for copy in fetches + loads:
+        copy.start()
+
+    barrier = pltpu.get_barrier_semaphore()
+    for by in range(1, tm):
+        pl.semaphore_signal(barrier, inc=1, device_id={"tm": lax.rem(z + by, tm)}, device_id_type=MESH)
+    for by in range(1, param):
+        pl.semaphore_signal(barrier, inc=1, device_id={"param": lax.rem(q + by, param)}, device_id_type=MESH)
+    pl.semaphore_wait(barrier, tm + param - 2)
+
+    def place(way, index):
+        return index if way == 0 else tm - 1 - index
+
+    def message(step, way, h, sender, act):
+        stage, slot = step // tm, step % tm
+        d = slot - sender
+        lanes = pl.ds(h * piece, piece)
+        peer = {"tm": jnp.clip(place(way, sender + 1), 0, tm - 1)}
+        there = (sender >= 0) & (sender < tm - 1)
+        if stage < chunks:
+            origin = jnp.clip(place(way, jnp.where(d < 0, -d, 0)), 0, tm - 1)
+
+            @pl.when(there & ((d < 0) | (d == 1)))
+            def _():
+                block = gathered.at[stage, origin, :, lanes]
+                copy = pltpu.make_async_remote_copy(
+                    src_ref=block, dst_ref=block, send_sem=a_send.at[way, stage, h, origin],
+                    recv_sem=a_recv.at[way, stage, h, origin], device_id=peer, device_id_type=MESH)
+                act(copy, None)
+
+        chunk = stage - 2
+        if 0 <= chunk < chunks:
+            owner = jnp.clip(place(way, jnp.where(d == 0, tm - 1, tm - d)), 0, tm - 1)
+
+            @pl.when(there & ((d == 0) | (d >= 2)))
+            def _():
+                copy = pltpu.make_async_remote_copy(
+                    src_ref=products.at[chunk, owner, :, lanes], dst_ref=arrived.at[way, chunk, owner, :, lanes],
+                    send_sem=b_send.at[way, chunk, h, owner], recv_sem=b_recv.at[way, chunk, h, owner],
+                    device_id=peer, device_id_type=MESH)
+
+                def add():
+                    products[chunk, owner, :, lanes] += arrived[way, chunk, owner, :, lanes]
+
+                act(copy, add)
+
+    def begin(copy, add):
+        copy.start()
+
+    def receive(copy, add):
+        copy.wait_recv()
+        if add is not None:
+            add()
+
+    def finish(copy, add):
+        copy.wait_send()
+
+    def prepare():
+        total = tm * epochs
+        source = lax.broadcasted_iota(jnp.int32, (total, total), 0)
+        target = lax.broadcasted_iota(jnp.int32, (total, total), 1)
+        blocks[...] = jnp.zeros_like(blocks)
+        for c in range(components):
+            row = jnp.broadcast_to(taps[c:c + 1, :total], (total, total))
+            shifted = pltpu.roll(row, 0, 1, stride=1, stride_axis=0)
+            shifted = jnp.where(target >= source, shifted, 0.0)
+            normal[...] = across(shifted, shifted, highest)
+            own = normal[pl.ds(pl.multiple_of(z * epochs, epochs), epochs), :]
+            span = slice(c * epochs, (c + 1) * epochs)
+            for other in range(tm):
+                blocks[other, span, span] = own[:, other * epochs:(other + 1) * epochs]
+
+    def convert():
+        for copy in loads:
+            copy.wait()
+
+        @pl.loop(0, tiles)
+        def _(j):
+            lanes = pl.ds(pl.multiple_of(j * tile, tile), tile)
+            high, low = halves(raw[:, lanes])
+            split[:rows, lanes] = high
+            split[rows:, lanes] = low
+
+    def to_param(c, by):
+        peer = {"param": lax.rem(q + by, param)}
+        return pltpu.make_async_remote_copy(
+            src_ref=partials.at[c, q], dst_ref=partials.at[c, q], send_sem=p_send.at[c, by],
+            recv_sem=p_recv.at[c, by], device_id=peer, device_id_type=MESH)
+
+    def to_tm(c, by):
+        peer = {"tm": lax.rem(z + by, tm)}
+        return pltpu.make_async_remote_copy(
+            src_ref=signals.at[c, z], dst_ref=signals.at[c, z], send_sem=t_send.at[c, by],
+            recv_sem=t_recv.at[c, by], device_id=peer, device_id_type=MESH)
+
+    def project(c):
+        columns = tm * CHUNK
+
+        def add(j, running):
+            lanes = pl.ds(pl.multiple_of(j * tile, tile), tile)
+            high, low = halves(gathered[c, :, :, lanes].reshape(columns, tile))
+            return running + across(jnp.concatenate([high, low], axis=0), split[:, lanes])
+
+        full = lax.fori_loop(0, tiles, add, jnp.zeros((2 * columns, 2 * rows), jnp.float32))
+        full = full[:columns] + full[columns:]
+        partials[c, q] = full[:, :rows] + full[:, rows:]
+        for by in range(1, param):
+            to_param(c, by).start()
+
+    def combine(c):
+        for by in range(1, param):
+            to_param(c, by).wait_recv()
+        total = partials[c, 0]
+        for other in range(1, param):
+            total = total + partials[c, other]
+        signals[c, z] = total
+        for by in range(1, tm):
+            to_tm(c, by).start()
+
+    def expand(c):
+        for by in range(1, tm):
+            to_tm(c, by).wait_recv()
+        weighted = across(signals[c, 0], blocks[0], highest)
+        for other in range(1, tm):
+            weighted = weighted + across(signals[c, other], blocks[other], highest)
+        columns = tm * CHUNK
+        high, low = halves(weighted)
+        both = jnp.concatenate([high, low], axis=0)
+
+        @pl.loop(0, tiles)
+        def _(j):
+            lanes = pl.ds(pl.multiple_of(j * tile, tile), tile)
+            first = jnp.dot(both, split[:rows, lanes], preferred_element_type=jnp.float32)
+            second = jnp.dot(high, split[rows:, lanes], preferred_element_type=jnp.float32)
+            value = first[:columns] + first[columns:] + second
+            products[c, :, :, lanes] = value.reshape(tm, CHUNK, tile)
+
+    def write(c):
+        return pltpu.make_async_copy(products.at[c, z], out.at[pl.ds(c * CHUNK, CHUNK)], out_sem.at[c])
+
+    steps = (chunks + 2) * tm
+    for step in range(steps + 1):
+        stage, slot = step // tm, step % tm
+        if slot == 0 and stage < chunks:
+            fetches[stage].wait()
+        for h in range(PIECES):
+            for way in range(2):
+                if step > 0:
+                    message(step - 1, way, h, place(way, z) - 1, receive)
+            for way in range(2):
+                if step < steps:
+                    message(step, way, h, place(way, z), begin)
+        if slot == 0 and stage >= 3:
+            write(stage - 3).start()
+        if step == 0:
+            prepare()
+            convert()
+        if 1 <= stage <= chunks:
+            for unit, work in enumerate((project, combine, expand)):
+                if slot == min(unit, tm - 1):
+                    work(stage - 1)
+
+    for step in range(steps):
+        for h in range(PIECES):
+            for way in range(2):
+                message(step, way, h, place(way, z), finish)
+    for c in range(chunks):
+        for by in range(1, param):
+            to_param(c, by).wait_send()
+        for by in range(1, tm):
+            to_tm(c, by).wait_send()
+        write(c).wait()
+
+
+def fused(tm, param, design, filter_taps, probes):
+    components, epochs, coefficients = design.shape
+    own = probes.shape[1]
+    chunks = own // CHUNK
+    rows = components * epochs
+    columns = tm * CHUNK
+    total = tm * epochs
+    f32 = jnp.float32
+    dma = pltpu.SemaphoreType.DMA
+    flops = 8 * rows * coefficients * own * tm
+    result = pl.pallas_call(
+        functools.partial(kernel, tm, param, components),
+        out_shape=jax.ShapeDtypeStruct((own, coefficients), f32),
+        in_specs=[pl.BlockSpec(memory_space=pl.ANY), pl.BlockSpec(memory_space=pltpu.VMEM), pl.BlockSpec(memory_space=pl.ANY)],
+        out_specs=pl.BlockSpec(memory_space=pl.ANY),
+        scratch_shapes=[
+            pltpu.VMEM((rows, coefficients), f32),
+            pltpu.VMEM((2 * rows, coefficients), jnp.bfloat16),
+            pltpu.VMEM((chunks, tm, CHUNK, coefficients), f32),
+            pltpu.VMEM((chunks, tm, CHUNK, coefficients), f32),
+            pltpu.VMEM((2, chunks, tm, CHUNK, coefficients), f32),
+            pltpu.VMEM((chunks, param, columns, rows), f32),
+            pltpu.VMEM((chunks, tm, columns, rows), f32),
+            pltpu.VMEM((total, total), f32),
+            pltpu.VMEM((tm, rows, rows), f32),
+            dma((coefficients // math.gcd(coefficients, 2048),)),
+            dma((chunks,)),
+            dma((chunks,)),
+            dma((2, chunks, PIECES, tm)),
+            dma((2, chunks, PIECES, tm)),
+            dma((2, chunks, PIECES, tm)),
+            dma((2, chunks, PIECES, tm)),
+            dma((chunks, param)),
+            dma((chunks, param)),
+            dma((chunks, tm)),
+            dma((chunks, tm)),
+        ],
+        compiler_params=pltpu.CompilerParams(collective_id=0, has_side_effects=True, vmem_limit_bytes=56 * 1024 * 1024),
+        cost_estimate=pl.CostEstimate(flops=flops, bytes_accessed=4 * coefficients * (rows + 2 * own), transcendentals=0),
+    )(design.reshape(rows, coefficients), filter_taps, probes.T)
+    return result.T
+
+
 def solution(mesh):
+    tm, param = mesh.shape["tm"], mesh.shape["param"]
+
+    def run(design, filter_taps, probes):
+        components, epochs, coefficients = design.shape
+        held = 4 * coefficients * (2 * components * epochs + 4 * probes.shape[1] * tm)
+        fits = held < 48 * 1024 * 1024 and tm * epochs <= min(filter_taps.shape[1], 512)
+        if fits and tm > 2 and param > 1 and probes.shape[1] % CHUNK == 0 and epochs % 8 == 0 and coefficients % 256 == 0:
+            return fused(tm, param, design, filter_taps, probes)
+        return body(design, filter_taps, probes)
+
     in_specs = (P(None, ("groups", "tm"), "param"), P(), P("param", ("groups", "tm")))
     out_specs = P("param", ("groups", "tm"))
-    return jax.shard_map(body, mesh=mesh, in_specs=in_specs, out_specs=out_specs, check_vma=False)
+    return jax.shard_map(run, mesh=mesh, in_specs=in_specs, out_specs=out_specs, check_vma=False)

time: 661 us -> 169 us (0.26)
  local copies, waits for them, and re-layouts: 289 us -> 2.46 us
  waiting for transfers between devices: 232 us -> 0 us
  Pallas kernels: 0 us -> 166 us
  matrix products: 89 us -> 0 us
  loops' own time: 14.6 us -> 0 us
  starting transfers between devices: 14.3 us -> 0 us
  between operations: 14.2 us -> 0.01 us
    gather x5 -> x0, local copies, waits for them, and re-layouts: 266 us -> none  [the longest x4 265 us: block_taps(): jnp.take(filter_taps, jnp.clip(lag_index, 0, tap_count - 1), axis=1)]
    pallas_call x0 -> x1, Pallas kernels: none -> 166 us  [fused(): pl.pallas_call(functools.partial(kernel, tm, param, components), out_shap...]
    unnamed x5 -> x0, waiting for transfers between devices: 121 us -> none
    all_gather x1 -> x0, waiting for transfers between devices: 102 us -> none  [body(): columns = lax.all_gather(probes, 'tm', axis=1, tiled=True)]
    dot_general x42 -> x0, matrix products: 89 us -> none  [the longest x20 55.6 us: block_product(): return jnp.einsum('ctp,ckt->pk', design_block, weighted, precision=highest)]
    another operation x2 -> x0, loops' own time: 14.6 us -> none  [the longest x1 14 us: body(): stacked = lax.map(block_product, jnp.arange(block_count, dtype=jnp.int32))]
    ppermute x8 -> x0, starting transfers between devices: 14.2 us -> none  [passed_along(): return lax.ppermute(value, axis, pairs)]
    dynamic_slice x20 -> x0, local copies, waits for them, and re-layouts: 13.2 us -> none  [body(): stacked = lax.map(block_product, jnp.arange(block_count, dtype=jnp.int32))]
  transfers between devices with their start and end apart: 11 -> 0, of which waited for: 6 -> 0; matrix products, arithmetic and copies ran while one was open for 41% -> 0% of each run, Pallas kernels for 0% -> 0%
where the time goes in v1:
time: 169 us; the launch traced here: 168 us
  Pallas kernels  166 us (98%)
  local copies, waits for them, and re-layouts  2.46 us (1%)
    pallas_call x1, Pallas kernels, fused(): pl.pallas_call(functools.partial(kernel, tm, param, components), out_shap...  166 us

profile of v1, /device:TPU:0, one launch (start us, length us, event | category | flops | bytes accessed | tf_op | source)
XLA Modules:
  0.0 168.5 jit_solution(1033036587777114556)
XLA Ops:
  0.0 166.0 %shard_map.37 = f32[32,10240]{1,0:T(8,128)} custom-call(f32[192,10240]{1,0:T(8,128)} %bitcast.3, f32[3,512]{1,0:T(4,128)} %taps.1, f32[32,10240]{1,0:T(8,128)} %bitcast.5), custom_call_target="tpu_custom_call" | custom-call | flops 2013265920 | bytes 10485760 | tf_op jit(solution)/shard_map/pallas_call | solution.py:294
  166.0 2.5 %copy.5 = f32[10240,32]{0,1:T(8,128)} copy(f32[10240,32]{0,1:T(8,128)} %bitcast.4) | data formatting | bytes 2621440

commit v2 on v1

--- a/solution.py
+++ b/solution.py
@@ -80,6 +80,8 @@
 
 CHUNK = 8
 PIECES = 2
+LAG = 2
+TILE = 1024
 MESH = pl.DeviceIdType.MESH
 
 
@@ -93,19 +95,73 @@
     return lax.dot_general(left, right, (((1,), (1,)), ((), ())), precision=precision, preferred_element_type=jnp.float32)
 
 
+def plan(tm, chunks):
+    links = tm - 1
+    units = 2 * PIECES + 1
+    todo = [[("a", c, h, i) for c in range(chunks) for h in range(PIECES) for i in range(link + 1)]
+            + [("b", c, h, i) for c in range(chunks) for h in range(PIECES) for i in range(link + 1, tm)]
+            for link in range(links)]
+    sent = [{} for _ in range(links)]
+    done = {}
+    slots, work = [], []
+
+    def rank(link, message):
+        kind, c, h, i = message
+        if kind == "a":
+            return 2 * c - 2 * (links - 1 - i) + link - i
+        return 5 + 8 * c - i + 2 * link
+
+    def passed(link, message, now):
+        return message in sent[link] and sent[link][message] + LAG <= now
+
+    def ready(link, message, now):
+        kind, c, h, i = message
+        if kind == "a":
+            return i == link or passed(link - 1, message, now)
+        return done.get((c, PIECES + 1 + h), now) < now and (link == 0 or passed(link - 1, message, now))
+
+    def possible(c, unit, now):
+        if (c, unit) in done or (unit > 0 and done.get((c, unit - 1), now) >= now):
+            return False
+        if unit >= PIECES:
+            return True
+        return all(passed(link, ("a", c, unit, i), now) for link in range(links) for i in range(link + 1))
+
+    while any(todo):
+        now = len(slots)
+        row = []
+        for link in range(links):
+            choice = [(rank(link, m), m) for m in todo[link] if ready(link, m, now)]
+            row.append(min(choice)[1] if choice else None)
+        for link, message in enumerate(row):
+            if message is not None:
+                sent[link][message] = now
+                todo[link].remove(message)
+        choice = [(c, unit) for c in range(chunks) for unit in range(units) if possible(c, unit, now)]
+        if choice:
+            done[min(choice)] = now
+        slots.append(row)
+        work.append(min(choice) if choice else None)
+    return slots, work
+
+
 def kernel(tm, param, components, design, taps, probes, out, raw, split, gathered, products, arrived, partials, signals,
-           normal, blocks, load_sem, probe_sem, out_sem, a_send, a_recv, b_send, b_recv, p_send, p_recv, t_send, t_recv):
+           weights, normal, blocks, load_sem, probe_sem, out_sem, a_send, a_recv, b_send, b_recv, p_send, p_recv, t_send,
+           t_recv):
     rows, coefficients = raw.shape
     epochs = rows // components
     chunks = gathered.shape[0]
+    columns = tm * CHUNK
     piece = coefficients // PIECES
     z = lax.axis_index("tm")
     q = lax.axis_index("param")
     highest = lax.Precision.HIGHEST
-
-    tile = math.gcd(coefficients, 2048)
+    slots, work = plan(tm, chunks)
+
+    tile = math.gcd(piece, TILE)
     tiles = coefficients // tile
-    loads = [pltpu.make_async_copy(design.at[:, pl.ds(j * tile, tile)], raw.at[:, pl.ds(j * tile, tile)], load_sem.at[j]) for j in range(tiles)]
+    steps_each = piece // tile
+    loads = [pltpu.make_async_copy(design.at[:, pl.ds(h * piece, piece)], raw.at[:, pl.ds(h * piece, piece)], load_sem.at[h]) for h in range(PIECES)]
     fetches = [pltpu.make_async_copy(probes.at[pl.ds(c * CHUNK, CHUNK)], gathered.at[c, z], probe_sem.at[c]) for c in range(chunks)]
     for copy in fetches + loads:
         copy.start()
@@ -120,64 +176,54 @@
     def place(way, index):
         return index if way == 0 else tm - 1 - index
 
-    def message(step, way, h, sender, act):
-        stage, slot = step // tm, step % tm
-        d = slot - sender
+    def transfer(way, link, message):
+        kind, c, h, i = message
         lanes = pl.ds(h * piece, piece)
-        peer = {"tm": jnp.clip(place(way, sender + 1), 0, tm - 1)}
-        there = (sender >= 0) & (sender < tm - 1)
-        if stage < chunks:
-            origin = jnp.clip(place(way, jnp.where(d < 0, -d, 0)), 0, tm - 1)
-
-            @pl.when(there & ((d < 0) | (d == 1)))
-            def _():
-                block = gathered.at[stage, origin, :, lanes]
-                copy = pltpu.make_async_remote_copy(
-                    src_ref=block, dst_ref=block, send_sem=a_send.at[way, stage, h, origin],
-                    recv_sem=a_recv.at[way, stage, h, origin], device_id=peer, device_id_type=MESH)
-                act(copy, None)
-
-        chunk = stage - 2
-        if 0 <= chunk < chunks:
-            owner = jnp.clip(place(way, jnp.where(d == 0, tm - 1, tm - d)), 0, tm - 1)
-
-            @pl.when(there & ((d == 0) | (d >= 2)))
-            def _():
-                copy = pltpu.make_async_remote_copy(
-                    src_ref=products.at[chunk, owner, :, lanes], dst_ref=arrived.at[way, chunk, owner, :, lanes],
-                    send_sem=b_send.at[way, chunk, h, owner], recv_sem=b_recv.at[way, chunk, h, owner],
-                    device_id=peer, device_id_type=MESH)
-
-                def add():
-                    products[chunk, owner, :, lanes] += arrived[way, chunk, owner, :, lanes]
-
-                act(copy, add)
-
-    def begin(copy, add):
-        copy.start()
-
-    def receive(copy, add):
-        copy.wait_recv()
-        if add is not None:
-            add()
-
-    def finish(copy, add):
-        copy.wait_send()
-
-    def prepare():
+        i = place(way, i)
+        if kind == "a":
+            source = target = gathered.at[c, i, :, lanes]
+            sems = a_send.at[way, c, h, i], a_recv.at[way, c, h, i]
+        else:
+            source, target = products.at[c, i, :, lanes], arrived.at[way, c, i, :, lanes]
+            sems = b_send.at[way, c, h, i], b_recv.at[way, c, h, i]
+        return pltpu.make_async_remote_copy(
+            src_ref=source, dst_ref=target, send_sem=sems[0], recv_sem=sems[1],
+            device_id={"tm": place(way, link + 1)}, device_id_type=MESH)
+
+    def each(row, act, ahead):
+        for way in range(2):
+            for link, message in enumerate(row):
+                if message is not None:
+                    pl.when(z == place(way, link + ahead))(functools.partial(act, way, link, message))
+
+    def begin(way, link, message):
+        transfer(way, link, message).start()
+
+    def finish(way, link, message):
+        transfer(way, link, message).wait_send()
+
+    def receive(way, link, message):
+        transfer(way, link, message).wait_recv()
+        kind, c, h, i = message
+        if kind == "b":
+            lanes = pl.ds(h * piece, piece)
+            i = place(way, i)
+            products[c, i, :, lanes] += arrived[way, c, i, :, lanes]
+
+    def prepare(c):
         total = tm * epochs
         source = lax.broadcasted_iota(jnp.int32, (total, total), 0)
         target = lax.broadcasted_iota(jnp.int32, (total, total), 1)
-        blocks[...] = jnp.zeros_like(blocks)
-        for c in range(components):
-            row = jnp.broadcast_to(taps[c:c + 1, :total], (total, total))
-            shifted = pltpu.roll(row, 0, 1, stride=1, stride_axis=0)
-            shifted = jnp.where(target >= source, shifted, 0.0)
-            normal[...] = across(shifted, shifted, highest)
-            own = normal[pl.ds(pl.multiple_of(z * epochs, epochs), epochs), :]
-            span = slice(c * epochs, (c + 1) * epochs)
-            for other in range(tm):
-                blocks[other, span, span] = own[:, other * epochs:(other + 1) * epochs]
+        if c == 0:
+            blocks[...] = jnp.zeros_like(blocks)
+        row = jnp.broadcast_to(taps[c:c + 1, :total], (total, total))
+        shifted = pltpu.roll(row, 0, 1, stride=1, stride_axis=0)
+        shifted = jnp.where(target >= source, shifted, 0.0)
+        normal[...] = across(shifted, shifted, highest)
+        own = normal[pl.ds(pl.multiple_of(z * epochs, epochs), epochs), :]
+        span = slice(c * epochs, (c + 1) * epochs)
+        for other in range(tm):
+            blocks[other, span, span] = own[:, other * epochs:(other + 1) * epochs]
 
     def convert():
         for copy in loads:
@@ -202,19 +248,20 @@
             src_ref=signals.at[c, z], dst_ref=signals.at[c, z], send_sem=t_send.at[c, by],
             recv_sem=t_recv.at[c, by], device_id=peer, device_id_type=MESH)
 
-    def project(c):
-        columns = tm * CHUNK
-
+    def project(c, h):
         def add(j, running):
             lanes = pl.ds(pl.multiple_of(j * tile, tile), tile)
             high, low = halves(gathered[c, :, :, lanes].reshape(columns, tile))
             return running + across(jnp.concatenate([high, low], axis=0), split[:, lanes])
 
-        full = lax.fori_loop(0, tiles, add, jnp.zeros((2 * columns, 2 * rows), jnp.float32))
+        full = jnp.zeros((2 * columns, 2 * rows), jnp.float32)
+        full = lax.fori_loop(h * steps_each, (h + 1) * steps_each, add, full)
         full = full[:columns] + full[columns:]
-        partials[c, q] = full[:, :rows] + full[:, rows:]
-        for by in range(1, param):
-            to_param(c, by).start()
+        value = full[:, :rows] + full[:, rows:]
+        partials[c, q] = value if h == 0 else partials[c, q] + value
+        if h == PIECES - 1:
+            for by in range(1, param):
+                to_param(c, by).start()
 
     def combine(c):
         for by in range(1, param):
@@ -226,53 +273,55 @@
         for by in range(1, tm):
             to_tm(c, by).start()
 
-    def expand(c):
-        for by in range(1, tm):
-            to_tm(c, by).wait_recv()
-        weighted = across(signals[c, 0], blocks[0], highest)
-        for other in range(1, tm):
-            weighted = weighted + across(signals[c, other], blocks[other], highest)
-        columns = tm * CHUNK
-        high, low = halves(weighted)
-        both = jnp.concatenate([high, low], axis=0)
-
-        @pl.loop(0, tiles)
+    def expand(c, h):
+        if h == 0:
+            for by in range(1, tm):
+                to_tm(c, by).wait_recv()
+            weighted = across(signals[c, 0], blocks[0], highest)
+            for other in range(1, tm):
+                weighted = weighted + across(signals[c, other], blocks[other], highest)
+            high, low = halves(weighted)
+            weights[...] = jnp.concatenate([high, low], axis=0)
+
+        @pl.loop(h * steps_each, (h + 1) * steps_each)
         def _(j):
             lanes = pl.ds(pl.multiple_of(j * tile, tile), tile)
-            first = jnp.dot(both, split[:rows, lanes], preferred_element_type=jnp.float32)
-            second = jnp.dot(high, split[rows:, lanes], preferred_element_type=jnp.float32)
+            first = jnp.dot(weights[...], split[:rows, lanes], preferred_element_type=jnp.float32)
+            second = jnp.dot(weights[:columns], split[rows:, lanes], preferred_element_type=jnp.float32)
             value = first[:columns] + first[columns:] + second
             products[c, :, :, lanes] = value.reshape(tm, CHUNK, tile)
 
     def write(c):
         return pltpu.make_async_copy(products.at[c, z], out.at[pl.ds(c * CHUNK, CHUNK)], out_sem.at[c])
 
-    steps = (chunks + 2) * tm
-    for step in range(steps + 1):
-        stage, slot = step // tm, step % tm
-        if slot == 0 and stage < chunks:
-            fetches[stage].wait()
-        for h in range(PIECES):
-            for way in range(2):
-                if step > 0:
-                    message(step - 1, way, h, place(way, z) - 1, receive)
-            for way in range(2):
-                if step < steps:
-                    message(step, way, h, place(way, z), begin)
-        if slot == 0 and stage >= 3:
-            write(stage - 3).start()
+    own_first = [min(g for g, row in enumerate(slots) if any(m is not None and m[:2] == ("a", c) for m in row)) for c in range(chunks)]
+    last = [max(g for g, row in enumerate(slots) if any(m is not None and m[:2] == ("b", c) for m in row)) for c in range(chunks)]
+    for step in range(len(slots) + LAG):
+        for c in range(chunks):
+            if own_first[c] == step:
+                fetches[c].wait()
+        if step >= LAG:
+            each(slots[step - LAG], receive, 1)
+        if step < len(slots):
+            each(slots[step], begin, 0)
+        for c in range(chunks):
+            if last[c] + LAG == step:
+                write(c).start()
         if step == 0:
-            prepare()
             convert()
-        if 1 <= stage <= chunks:
-            for unit, work in enumerate((project, combine, expand)):
-                if slot == min(unit, tm - 1):
-                    work(stage - 1)
-
-    for step in range(steps):
-        for h in range(PIECES):
-            for way in range(2):
-                message(step, way, h, place(way, z), finish)
+        elif step <= components:
+            prepare(step - 1)
+        if step < len(slots) and work[step] is not None:
+            c, unit = work[step]
+            if unit < PIECES:
+                project(c, unit)
+            elif unit == PIECES:
+                combine(c)
+            else:
+                expand(c, unit - PIECES - 1)
+
+    for row in slots:
+        each(row, finish, 0)
     for c in range(chunks):
         for by in range(1, param):
             to_param(c, by).wait_send()
@@ -304,9 +353,10 @@
             pltpu.VMEM((2, chunks, tm, CHUNK, coefficients), f32),
             pltpu.VMEM((chunks, param, columns, rows), f32),
             pltpu.VMEM((chunks, tm, columns, rows), f32),
+            pltpu.VMEM((2 * columns, rows), jnp.bfloat16),
             pltpu.VMEM((total, total), f32),
             pltpu.VMEM((tm, rows, rows), f32),
-            dma((coefficients // math.gcd(coefficients, 2048),)),
+            dma((PIECES,)),
             dma((chunks,)),
             dma((chunks,)),
             dma((2, chunks, PIECES, tm)),

time: 169 us -> 143 us (0.85)
  Pallas kernels: 166 us -> 140 us
    pallas_call x1, Pallas kernels: 166 us -> 140 us  [fused(): pl.pallas_call(functools.partial(kernel, tm, param, components), out_shap...]
where the time goes in v2:
time: 143 us; the launch traced here: 142 us
  Pallas kernels  140 us (98%)
  local copies, waits for them, and re-layouts  2.46 us (2%)
    pallas_call x1, Pallas kernels, fused(): pl.pallas_call(functools.partial(kernel, tm, param, components), out_shap...  140 us

profile of v2, /device:TPU:0, one launch (start us, length us, event | category | flops | bytes accessed | tf_op | source)
XLA Modules:
  0.0 142.4 jit_solution(11466049977028510854)
XLA Ops:
  0.0 139.9 %shard_map.37 = f32[32,10240]{1,0:T(8,128)} custom-call(f32[192,10240]{1,0:T(8,128)} %bitcast.3, f32[3,512]{1,0:T(4,128)} %taps.1, f32[32,10240]{1,0:T(8,128)} %bitcast.5), custom_call_target="tpu_custom_call" | custom-call | flops 2013265920 | bytes 10485760 | tf_op jit(solution)/shard_map/pallas_call | solution.py:343
  139.9 2.5 %copy.5 = f32[10240,32]{0,1:T(8,128)} copy(f32[10240,32]{0,1:T(8,128)} %bitcast.4) | data formatting | bytes 2621440

commit v3 on v2

--- a/solution.py
+++ b/solution.py
@@ -79,9 +79,12 @@
 
 
 CHUNK = 8
-PIECES = 2
-LAG = 2
-TILE = 1024
+PIECES = 4
+LAG = 4
+GAPS = 1, 3, 1
+TILE = 1280
+WA = 2, -2, 1
+WB = 5, 8, -1, 2
 MESH = pl.DeviceIdType.MESH
 
 
@@ -97,7 +100,7 @@
 
 def plan(tm, chunks):
     links = tm - 1
-    units = 2 * PIECES + 1
+    units = 2 * PIECES + 2
     todo = [[("a", c, h, i) for c in range(chunks) for h in range(PIECES) for i in range(link + 1)]
             + [("b", c, h, i) for c in range(chunks) for h in range(PIECES) for i in range(link + 1, tm)]
             for link in range(links)]
@@ -108,8 +111,8 @@
     def rank(link, message):
         kind, c, h, i = message
         if kind == "a":
-            return 2 * c - 2 * (links - 1 - i) + link - i
-        return 5 + 8 * c - i + 2 * link
+            return WA[0] * c + WA[1] * (links - 1 - i) + WA[2] * (link - i)
+        return WB[0] + WB[1] * c + WB[2] * i + WB[3] * link
 
     def passed(link, message, now):
         return message in sent[link] and sent[link][message] + LAG <= now
@@ -118,10 +121,11 @@
         kind, c, h, i = message
         if kind == "a":
             return i == link or passed(link - 1, message, now)
-        return done.get((c, PIECES + 1 + h), now) < now and (link == 0 or passed(link - 1, message, now))
+        return done.get((c, PIECES + 2 + h), now) < now and (link == 0 or passed(link - 1, message, now))
 
     def possible(c, unit, now):
-        if (c, unit) in done or (unit > 0 and done.get((c, unit - 1), now) >= now):
+        wait = GAPS[unit - PIECES] if PIECES <= unit <= PIECES + 2 else 1
+        if (c, unit) in done or (unit > 0 and done.get((c, unit - 1), now) + wait > now):
             return False
         if unit >= PIECES:
             return True
@@ -145,13 +149,14 @@
     return slots, work
 
 
-def kernel(tm, param, components, design, taps, probes, out, raw, split, gathered, products, arrived, partials, signals,
-           weights, normal, blocks, load_sem, probe_sem, out_sem, a_send, a_recv, b_send, b_recv, p_send, p_recv, t_send,
-           t_recv):
+def kernel(tm, param, components, design, taps, probes, out, raw, split, gathered, products, arrived, mine, partials,
+           signals, filtered, weights, normal, blocks, load_sem, probe_sem, out_sem, z_send, z_recv, p_send, p_recv, t_send,
+           t_recv, f_send, f_recv):
     rows, coefficients = raw.shape
     epochs = rows // components
     chunks = gathered.shape[0]
     columns = tm * CHUNK
+    share = columns // param
     piece = coefficients // PIECES
     z = lax.axis_index("tm")
     q = lax.axis_index("param")
@@ -182,12 +187,10 @@
         i = place(way, i)
         if kind == "a":
             source = target = gathered.at[c, i, :, lanes]
-            sems = a_send.at[way, c, h, i], a_recv.at[way, c, h, i]
         else:
             source, target = products.at[c, i, :, lanes], arrived.at[way, c, i, :, lanes]
-            sems = b_send.at[way, c, h, i], b_recv.at[way, c, h, i]
         return pltpu.make_async_remote_copy(
-            src_ref=source, dst_ref=target, send_sem=sems[0], recv_sem=sems[1],
+            src_ref=source, dst_ref=target, send_sem=z_send.at[way, c, h, i], recv_sem=z_recv.at[way, c, h, i],
             device_id={"tm": place(way, link + 1)}, device_id_type=MESH)
 
     def each(row, act, ahead):
@@ -237,10 +240,16 @@
             split[rows:, lanes] = low
 
     def to_param(c, by):
+        other = lax.rem(q + by, param)
+        return pltpu.make_async_remote_copy(
+            src_ref=mine.at[c, other], dst_ref=partials.at[c, q], send_sem=p_send.at[c, by],
+            recv_sem=p_recv.at[c, by], device_id={"param": other}, device_id_type=MESH)
+
+    def to_all(c, by):
         peer = {"param": lax.rem(q + by, param)}
         return pltpu.make_async_remote_copy(
-            src_ref=partials.at[c, q], dst_ref=partials.at[c, q], send_sem=p_send.at[c, by],
-            recv_sem=p_recv.at[c, by], device_id=peer, device_id_type=MESH)
+            src_ref=filtered.at[c, q], dst_ref=filtered.at[c, q], send_sem=f_send.at[c, by],
+            recv_sem=f_recv.at[c, by], device_id=peer, device_id_type=MESH)
 
     def to_tm(c, by):
         peer = {"tm": lax.rem(z + by, tm)}
@@ -257,9 +266,10 @@
         full = jnp.zeros((2 * columns, 2 * rows), jnp.float32)
         full = lax.fori_loop(h * steps_each, (h + 1) * steps_each, add, full)
         full = full[:columns] + full[columns:]
-        value = full[:, :rows] + full[:, rows:]
-        partials[c, q] = value if h == 0 else partials[c, q] + value
+        value = (full[:, :rows] + full[:, rows:]).reshape(param, share, rows)
+        mine[c] = value if h == 0 else mine[c] + value
         if h == PIECES - 1:
+            partials[c, q] = mine[c, q]
             for by in range(1, param):
                 to_param(c, by).start()
 
@@ -273,14 +283,21 @@
         for by in range(1, tm):
             to_tm(c, by).start()
 
+    def weigh(c):
+        for by in range(1, tm):
+            to_tm(c, by).wait_recv()
+        weighted = across(signals[c, 0], blocks[0], highest)
+        for other in range(1, tm):
+            weighted = weighted + across(signals[c, other], blocks[other], highest)
+        filtered[c, q] = weighted
+        for by in range(1, param):
+            to_all(c, by).start()
+
     def expand(c, h):
         if h == 0:
-            for by in range(1, tm):
-                to_tm(c, by).wait_recv()
-            weighted = across(signals[c, 0], blocks[0], highest)
-            for other in range(1, tm):
-                weighted = weighted + across(signals[c, other], blocks[other], highest)
-            high, low = halves(weighted)
+            for by in range(1, param):
+                to_all(c, by).wait_recv()
+            high, low = halves(filtered[c].reshape(columns, rows))
             weights[...] = jnp.concatenate([high, low], axis=0)
 
         @pl.loop(h * steps_each, (h + 1) * steps_each)
@@ -304,6 +321,8 @@
             each(slots[step - LAG], receive, 1)
         if step < len(slots):
             each(slots[step], begin, 0)
+        if step >= LAG:
+            each(slots[step - LAG], finish, 0)
         for c in range(chunks):
             if last[c] + LAG == step:
                 write(c).start()
@@ -317,14 +336,14 @@
                 project(c, unit)
             elif unit == PIECES:
                 combine(c)
+            elif unit == PIECES + 1:
+                weigh(c)
             else:
-                expand(c, unit - PIECES - 1)
-
-    for row in slots:
-        each(row, finish, 0)
+                expand(c, unit - PIECES - 2)
     for c in range(chunks):
         for by in range(1, param):
             to_param(c, by).wait_send()
+            to_all(c, by).wait_send()
         for by in range(1, tm):
             to_tm(c, by).wait_send()
         write(c).wait()
@@ -336,6 +355,7 @@
     chunks = own // CHUNK
     rows = components * epochs
     columns = tm * CHUNK
+    share = columns // param
     total = tm * epochs
     f32 = jnp.float32
     dma = pltpu.SemaphoreType.DMA
@@ -351,8 +371,10 @@
             pltpu.VMEM((chunks, tm, CHUNK, coefficients), f32),
             pltpu.VMEM((chunks, tm, CHUNK, coefficients), f32),
             pltpu.VMEM((2, chunks, tm, CHUNK, coefficients), f32),
-            pltpu.VMEM((chunks, param, columns, rows), f32),
-            pltpu.VMEM((chunks, tm, columns, rows), f32),
+            pltpu.VMEM((chunks, param, share, rows), f32),
+            pltpu.VMEM((chunks, param, share, rows), f32),
+            pltpu.VMEM((chunks, tm, share, rows), f32),
+            pltpu.VMEM((chunks, param, share, rows), f32),
             pltpu.VMEM((2 * columns, rows), jnp.bfloat16),
             pltpu.VMEM((total, total), f32),
             pltpu.VMEM((tm, rows, rows), f32),
@@ -361,12 +383,12 @@
             dma((chunks,)),
             dma((2, chunks, PIECES, tm)),
             dma((2, chunks, PIECES, tm)),
-            dma((2, chunks, PIECES, tm)),
-            dma((2, chunks, PIECES, tm)),
             dma((chunks, param)),
             dma((chunks, param)),
             dma((chunks, tm)),
             dma((chunks, tm)),
+            dma((chunks, param)),
+            dma((chunks, param)),
         ],
         compiler_params=pltpu.CompilerParams(collective_id=0, has_side_effects=True, vmem_limit_bytes=56 * 1024 * 1024),
         cost_estimate=pl.CostEstimate(flops=flops, bytes_accessed=4 * coefficients * (rows + 2 * own), transcendentals=0),
@@ -381,7 +403,7 @@
         components, epochs, coefficients = design.shape
         held = 4 * coefficients * (2 * components * epochs + 4 * probes.shape[1] * tm)
         fits = held < 48 * 1024 * 1024 and tm * epochs <= min(filter_taps.shape[1], 512)
-        if fits and tm > 2 and param > 1 and probes.shape[1] % CHUNK == 0 and epochs % 8 == 0 and coefficients % 256 == 0:
+        if fits and tm > 2 and param > 1 and probes.shape[1] % CHUNK == 0 and epochs % 8 == 0 and coefficients % (128 * PIECES) == 0 and tm * CHUNK % (8 * param) == 0:
             return fused(tm, param, design, filter_taps, probes)
         return body(design, filter_taps, probes)
 

time: 143 us -> 138 us (0.965)
  Pallas kernels: 140 us -> 135 us
    pallas_call x1, Pallas kernels: 140 us -> 135 us  [fused(): pl.pallas_call(functools.partial(kernel, tm, param, components), out_shap...]
where the time goes in v3:
time: 138 us; the launch traced here: 137 us
  Pallas kernels  135 us (98%)
  local copies, waits for them, and re-layouts  2.46 us (2%)
    pallas_call x1, Pallas kernels, fused(): pl.pallas_call(functools.partial(kernel, tm, param, components), out_shap...  135 us

profile of v3, /device:TPU:0, one launch (start us, length us, event | category | flops | bytes accessed | tf_op | source)
XLA Modules:
  0.0 137.5 jit_solution(10444078852328708290)
XLA Ops:
  0.0 135.0 %shard_map.37 = f32[32,10240]{1,0:T(8,128)} custom-call(f32[192,10240]{1,0:T(8,128)} %bitcast.3, f32[3,512]{1,0:T(4,128)} %taps.1, f32[32,10240]{1,0:T(8,128)} %bitcast.5), custom_call_target="tpu_custom_call" | custom-call | flops 2013265920 | bytes 10485760 | tf_op jit(solution)/shard_map/pallas_call | solution.py:363
  135.0 2.5 %copy.5 = f32[10240,32]{0,1:T(8,128)} copy(f32[10240,32]{0,1:T(8,128)} %bitcast.4) | data formatting | bytes 2621440
